TPU v7x, 32 devices: a whole 2x2x4 slice. The times are simulated.
32 devices in a mesh: ctx: 8 (over z, x), tp: 4 (over y, core).
Axes of the slice: x: 2, y: 2, z: 4, core: 2. Of those that a mesh axis runs over, the one named last changes fastest.
Arguments:
- hidden_in: bfloat16 [2, 1024, 1024], P(None, 'ctx'), may hold values from -6 to 6
- seg_ids: int32 [2, 1024], replicated, may hold values from 0 to 4, as said below
- first_gain: float32 [1024], replicated, may hold values from 0.5 to 1.5
- query_weight: bfloat16 [1024, 1024], P(None, 'tp'), may hold values from -0.1875 to 0.1875
- keyval_weight: bfloat16 [1024, 512], replicated, may hold values from -0.1875 to 0.1875
- attn_out_weight: bfloat16 [1024, 1024], P('tp'), may hold values from -0.75 to 0.75
- mixin_weight: bfloat16 [1024, 1536], P(None, 'tp'), may hold values from -0.1875 to 0.1875
- mixgate_weight: bfloat16 [1024, 1536], P(None, 'tp'), may hold values from -0.1875 to 0.1875
- inject_weight: bfloat16 [1024, 128], replicated, may hold values from -0.00390625 to 0.00390625
- readout_weight: bfloat16 [1024, 128], replicated, may hold values from -0.1875 to 0.1875
- step_weight: bfloat16 [1024, 24], P(None, 'tp'), may hold values from -0.1875 to 0.1875
- step_bias: float32 [24], P('tp'), may hold values from -1 to 1
- decay_rate: float32 [24], P('tp'), may hold values from 0.00029296876 to 0.06
- skip_gain: float32 [24], P('tp'), may hold values from 0.5 to 1.5
- mixout_weight: bfloat16 [1536, 1024], P('tp'), may hold values from -0.15625 to 0.15625
- second_gain: float32 [1024], replicated, may hold values from 0.5 to 1.5
- gate_weight: bfloat16 [1024, 2048], P(None, 'tp'), may hold values from -0.1875 to 0.1875
- up_weight: bfloat16 [1024, 2048], P(None, 'tp'), may hold values from -0.1875 to 0.1875
- down_weight: bfloat16 [2048, 1024], P('tp'), may hold values from -0.125 to 0.125
- cotangent: bfloat16 [2, 1024, 1024], P(None, 'ctx'), may hold values from -6 to 6
Outputs:
- layer_out: bfloat16 [2, 1024, 1024], P(None, 'ctx')
- grad_hidden: float32 [2, 1024, 1024], P(None, 'ctx')
- grad_first_gain: float32 [1024], replicated
- grad_query: float32 [1024, 1024], P('ctx', 'tp')
- grad_keyval: float32 [1024, 512], P(('ctx', 'tp'))
- grad_attn_out: float32 [1024, 1024], P('tp', 'ctx')
- grad_mixin: float32 [1024, 1536], P('ctx', 'tp')
- grad_mixgate: float32 [1024, 1536], P('ctx', 'tp')
- grad_inject: float32 [1024, 128], P(('ctx', 'tp'))
- grad_readout: float32 [1024, 128], P(('ctx', 'tp'))
- grad_step: float32 [1024, 24], P('ctx', 'tp')
- grad_step_bias: float32 [24], P('tp')
- grad_decay_rate: float32 [24], P('tp')
- grad_skip_gain: float32 [24], P('tp')
- grad_mixout: float32 [1536, 1024], P('tp', 'ctx')
- grad_second_gain: float32 [1024], replicated
- grad_gate: float32 [1024, 2048], P('ctx', 'tp')
- grad_up: float32 [1024, 2048], P('ctx', 'tp')
- grad_down: float32 [2048, 1024], P('tp', 'ctx')
Inputs may be any that keep to these rules, and one draw needn't show every extreme that they name: `seg_ids`: within each sequence the ids never fall and start at 0; in one sequence of each draw all ids are 0, in every other one the last position has id 4.
All inputs are finite; a program needn't handle non-finite values.
Results may differ from a plain program's by a relative error of at most 0.025.
Values may be sent and summed in bfloat16 or wider, within the bound.
A program may use at most 128 MiB of HBM per device.

v0:
```python
import math

import jax
import jax.numpy as jnp
from jax import lax
from jax.sharding import PartitionSpec as P

QHEADS = 8
KVHEADS = 2
HEAD = 128


NORM_EPS = 1e-05
MASK_FILL = -1e30
FAR_BELOW = -10000.0
exact_precision = lax.Precision.HIGHEST


def carried_in(array, axis, combine, identity, reverse):
    peers, index = (lax.axis_size(axis), lax.axis_index(axis))
    everything = jax.tree.map(
        lambda part, kind: lax.all_gather(part.astype(kind), axis),
        array,
        jax.tree.map(lambda a: jnp.bfloat16 if a.dtype == jnp.float32 else a.dtype, array),
    )
    start = jax.tree.map(
        lambda part, zero: jnp.broadcast_to(jnp.asarray(zero, part.dtype), part.shape),
        array,
        identity,
    )

    def step(k, before):
        at = peers - 1 - k if reverse else k
        reached = at > index if reverse else at < index
        new = combine(
            before, jax.tree.map(lambda part, own: part[at].astype(own.dtype), everything, array)
        )
        return jax.tree.map(lambda a, b: jnp.where(reached, a, b), new, before)

    return lax.fori_loop(0, peers, step, start)


def decays(step_raw, decay_rate):
    step_size = jax.nn.softplus(step_raw)
    return (step_size, jnp.cumsum(-decay_rate[None, :] * step_size, axis=0))


def state_part(mix_in, key_vec, step_size, log_decay, seg_here, seg_before):
    log_end = log_decay[-1]
    same_end = (seg_here == seg_here[-1]).astype(jnp.float32)
    end_weight = jnp.exp(log_end[None, :] - log_decay) * same_end[:, None] * step_size
    state = jnp.einsum("sh,shp,sn->hpn", end_weight, mix_in, key_vec, precision=exact_precision)
    carried = jnp.exp(log_end) * (seg_here[-1] == seg_before).astype(jnp.float32)
    return (carried, state)


def out_part(
    mix_in, key_vec, read_vec, step_size, log_decay, skip_gain, seg_here, seg_before, state_in
):
    places = jnp.arange(seg_here.shape[0], dtype=jnp.int32)
    visible = (places[:, None] >= places[None, :]) & (seg_here[:, None] == seg_here[None, :])
    log_gap = log_decay[:, None, :] - log_decay[None, :, :]
    weights = jnp.exp(jnp.where(visible[:, :, None], log_gap, FAR_BELOW)) * step_size[None, :, :]
    mixing = jnp.einsum("tn,sn->ts", read_vec, key_vec, precision=exact_precision)
    result = jnp.einsum(
        "tsh,shp->thp", weights * mixing[:, :, None], mix_in, precision=exact_precision
    )
    entry = jnp.exp(log_decay) * (seg_here == seg_before).astype(jnp.float32)[:, None]
    result = result + entry[:, :, None] * jnp.einsum(
        "tn,hpn->thp", read_vec, state_in, precision=exact_precision
    )
    return result + skip_gain[None, :, None] * mix_in


def block_scan(
    mix_in, key_vec, read_vec, step_raw, decay_rate, skip_gain, seg_here, seg_before, state_in
):
    step_size, log_decay = decays(step_raw, decay_rate)
    carried, state = state_part(mix_in, key_vec, step_size, log_decay, seg_here, seg_before)
    result = out_part(
        mix_in, key_vec, read_vec, step_size, log_decay, skip_gain, seg_here, seg_before, state_in
    )
    return (result, carried, state)


def over_blocks(function, axes):
    return jax.vmap(jax.vmap(function, in_axes=axes), in_axes=axes)


def compose(earlier, later):
    return (earlier[0] * later[0], later[0][..., None, None] * earlier[1] + later[1])


def choose(flag, first, other):
    return jax.tree.map(lambda left, right: jnp.where(flag, left, right), first, other)


def rms_scale(value_rows):
    return lax.rsqrt(jnp.mean(value_rows * value_rows, axis=-1, keepdims=True) + NORM_EPS)


def norm_back(d_norm, gain, value_rows, scale):
    d_hat = d_norm * gain
    return scale * d_hat - value_rows * scale**3 * jnp.mean(
        d_hat * value_rows, axis=-1, keepdims=True
    )


def times_trans(grad, weight_matrix):
    return lax.dot_general(
        grad,
        weight_matrix,
        (((grad.ndim - 1,), (1,)), ((), ())),
        preferred_element_type=jnp.float32,
    )


def outer_rows(left, right):
    return lax.dot_general(
        left, right, (((0, 1), (0, 1)), ((), ())), preferred_element_type=jnp.float32
    )


def body(
    hidden_in,
    seg_ids,
    first_gain,
    query_weight,
    keyval_weight,
    attn_out_weight,
    mixin_weight,
    mixgate_weight,
    inject_weight,
    readout_weight,
    step_weight,
    step_bias,
    decay_rate,
    skip_gain,
    mixout_weight,
    second_gain,
    gate_weight,
    up_weight,
    down_weight,
    cotangent,
):
    ctx_size = lax.axis_size("ctx")
    ctx_index = lax.axis_index("ctx")
    tp_index = lax.axis_index("tp")
    seq_count, row_count, width = hidden_in.shape
    block_rows = row_count // 2
    seq_length = 2 * ctx_size * block_rows
    q_local = query_weight.shape[1] // HEAD
    heads_local = step_weight.shape[1]
    mamba_head = mixin_weight.shape[1] // heads_local
    kv_head = tp_index * q_local // (QHEADS // KVHEADS)
    scale = HEAD ** (-0.5)
    last_dev = ctx_index == ctx_size - 1

    def positions(device, local):
        return jnp.where(
            local < block_rows,
            device * block_rows + local,
            (2 * ctx_size - 1 - device) * block_rows + local - block_rows,
        )

    local_rows = jnp.arange(row_count, dtype=jnp.int32)
    q_places = positions(ctx_index, local_rows)
    q_segs = jnp.take(seg_ids, q_places, axis=1)
    all_rows = jnp.arange(seq_length, dtype=jnp.int32)
    k_places = positions(all_rows // row_count, all_rows % row_count)
    k_segs = jnp.take(seg_ids, k_places, axis=1)
    hidden = hidden_in.astype(jnp.float32)
    first_scale = rms_scale(hidden)
    normed = (hidden * first_scale * first_gain).astype(jnp.bfloat16)
    queries = jnp.dot(normed, query_weight, preferred_element_type=jnp.float32).astype(jnp.bfloat16)
    queries = queries.reshape(seq_count, row_count, q_local, HEAD)
    keyval_mine = lax.dynamic_slice_in_dim(keyval_weight, kv_head * 2 * HEAD, 2 * HEAD, 1)
    keyval = jnp.dot(normed, keyval_mine, preferred_element_type=jnp.float32).astype(jnp.bfloat16)
    keyval_all = lax.all_gather(keyval, "ctx", axis=1, tiled=True)
    key_block = math.gcd(seq_length, 512)
    key_steps = seq_length // key_block

    def scored(keys, step_idx):
        raw = (
            jnp.einsum("srhd,skd->srhk", queries, keys, preferred_element_type=jnp.float32) * scale
        )
        places = lax.dynamic_slice_in_dim(k_places, step_idx * key_block, key_block, 0)
        segs = lax.dynamic_slice_in_dim(k_segs, step_idx * key_block, key_block, 1)
        visible = (places[None, None, :] <= q_places[None, :, None]) & (
            segs[:, None, :] == q_segs[:, :, None]
        )
        return jnp.where(visible[:, :, None, :], raw, MASK_FILL)

    def attend(step_idx, carry):
        running, total, accum = carry
        block_kv = lax.dynamic_slice_in_dim(keyval_all, step_idx * key_block, key_block, 1)
        scores = scored(block_kv[..., :HEAD], step_idx)
        newmax = jnp.maximum(running, jnp.max(scores, axis=-1))
        factor = jnp.exp(running - newmax)
        probs = jnp.exp(scores - newmax[..., None])
        total = total * factor + jnp.sum(probs, axis=-1)
        accum = accum * factor[..., None] + jnp.einsum(
            "srhk,skd->srhd",
            probs.astype(jnp.bfloat16),
            block_kv[..., HEAD:],
            preferred_element_type=jnp.float32,
        )
        return (newmax, total, accum)

    start = (
        jnp.full((seq_count, row_count, q_local), MASK_FILL, jnp.float32),
        jnp.zeros((seq_count, row_count, q_local), jnp.float32),
        jnp.zeros((seq_count, row_count, q_local, HEAD), jnp.float32),
    )
    running, total, accum = lax.fori_loop(0, key_steps, attend, start)
    attn_full = accum / total[..., None]
    log_total = running + jnp.log(total)
    attn_low = attn_full.astype(jnp.bfloat16).reshape(seq_count, row_count, q_local * HEAD)
    mix_in = jnp.dot(normed, mixin_weight, preferred_element_type=jnp.float32).astype(jnp.bfloat16)
    mix_gate = jnp.dot(normed, mixgate_weight, preferred_element_type=jnp.float32)
    key_vec = jnp.dot(normed, inject_weight, preferred_element_type=jnp.float32).astype(
        jnp.bfloat16
    )
    read_vec = jnp.dot(normed, readout_weight, preferred_element_type=jnp.float32).astype(
        jnp.bfloat16
    )
    step_raw = jnp.dot(normed, step_weight, preferred_element_type=jnp.float32) + step_bias

    def blocked(value_rows, tail):
        return value_rows.reshape((seq_count, 2, block_rows) + tail)

    n_state = key_vec.shape[-1]
    mix_blocks = blocked(mix_in.astype(jnp.float32), (heads_local, mamba_head))
    key_blocks = blocked(key_vec.astype(jnp.float32), (n_state,))
    read_blocks = blocked(read_vec.astype(jnp.float32), (n_state,))
    step_blocks = blocked(step_raw, (heads_local,))
    seg_blocks = blocked(q_segs, ())
    first_before = jnp.where(
        ctx_index == 0,
        -1,
        lax.dynamic_index_in_dim(
            seg_ids, jnp.maximum(ctx_index * block_rows - 1, 0), 1, keepdims=False
        ),
    )
    second_before = lax.dynamic_index_in_dim(
        seg_ids, (2 * ctx_size - 1 - ctx_index) * block_rows - 1, 1, keepdims=False
    )
    seg_before = jnp.stack([first_before, second_before], axis=1)
    step_size, log_decay = over_blocks(decays, (0, None))(step_blocks, decay_rate)
    carried, state = over_blocks(state_part, (0, 0, 0, 0, 0, 0))(
        mix_blocks, key_blocks, step_size, log_decay, seg_blocks, seg_before
    )
    first_elem = (carried[:, 0], state[:, 0])
    second_elem = (carried[:, 1], state[:, 1])
    identity = (jnp.ones_like(carried[:, 0]), jnp.zeros_like(state[:, 0]))
    rise = carried_in(first_elem, "ctx", compose, identity, False)
    first_total = compose(rise, first_elem)
    fall_in = choose(last_dev, compose(first_total, second_elem), second_elem)
    fall = carried_in(fall_in, "ctx", compose, identity, True)
    state_in = jnp.stack([rise[1], jnp.where(last_dev, first_total[1], fall[1])], axis=1)
    mixed = over_blocks(out_part, (0, 0, 0, 0, 0, None, 0, 0, 0))(
        mix_blocks,
        key_blocks,
        read_blocks,
        step_size,
        log_decay,
        skip_gain,
        seg_blocks,
        seg_before,
        state_in,
    )
    mixed = mixed.reshape(seq_count, row_count, heads_local * mamba_head)
    gate_act = jax.nn.silu(mix_gate)
    gated = (mixed * gate_act).astype(jnp.bfloat16)
    branch = lax.psum(
        (
            jnp.dot(attn_low, attn_out_weight, preferred_element_type=jnp.float32)
            + jnp.dot(gated, mixout_weight, preferred_element_type=jnp.float32)
        ).astype(jnp.bfloat16),
        "tp",
    ).astype(jnp.float32)
    middle = hidden + branch
    second_scale = rms_scale(middle)
    normed_two = (middle * second_scale * second_gain).astype(jnp.bfloat16)
    gate = jnp.dot(normed_two, gate_weight, preferred_element_type=jnp.float32)
    up_val = jnp.dot(normed_two, up_weight, preferred_element_type=jnp.float32)
    gate_sig = jax.nn.sigmoid(gate)
    inner = (gate * gate_sig * up_val).astype(jnp.bfloat16)
    mlp_out = lax.psum(
        jnp.dot(inner, down_weight, preferred_element_type=jnp.float32).astype(jnp.bfloat16), "tp"
    ).astype(jnp.float32)
    layer_out = (middle + mlp_out).astype(jnp.bfloat16)
    inner_gradient = times_trans(cotangent, down_weight)
    grad_down = outer_rows(inner, cotangent)
    d_gate = (inner_gradient * up_val * gate_sig * (1.0 + gate * (1.0 - gate_sig))).astype(
        jnp.bfloat16
    )
    d_up = (inner_gradient * gate * gate_sig).astype(jnp.bfloat16)
    grad_gate = outer_rows(normed_two, d_gate)
    grad_up = outer_rows(normed_two, d_up)
    second_normed_gradient = lax.psum(
        (times_trans(d_gate, gate_weight) + times_trans(d_up, up_weight)).astype(jnp.bfloat16), "tp"
    ).astype(jnp.float32)
    grad_second = jnp.sum(second_normed_gradient * middle * second_scale, axis=(0, 1))
    d_middle = cotangent.astype(jnp.float32) + norm_back(
        second_normed_gradient, second_gain, middle, second_scale
    )
    d_branch = d_middle.astype(jnp.bfloat16)
    grad_attn_out = outer_rows(attn_low, d_branch)
    grad_mixout = outer_rows(gated, d_branch)
    d_attn = (
        times_trans(d_branch, attn_out_weight)
        .astype(jnp.bfloat16)
        .reshape(seq_count, row_count, q_local, HEAD)
    )
    d_gated = times_trans(d_branch, mixout_weight).astype(jnp.bfloat16).astype(jnp.float32)
    d_mixed = d_gated * gate_act
    mixgate_sig = jax.nn.sigmoid(mix_gate)
    d_mix_gate = (d_gated * mixed * mixgate_sig * (1.0 + mix_gate * (1.0 - mixgate_sig))).astype(
        jnp.bfloat16
    )
    delta = jnp.sum(d_attn.astype(jnp.float32) * attn_full, axis=-1)

    def query_grad(block_kv, step_idx):
        probs = jnp.exp(scored(block_kv[..., :HEAD], step_idx) - log_total[..., None])
        probability_gradient = jnp.einsum(
            "srhd,skd->srhk", d_attn, block_kv[..., HEAD:], preferred_element_type=jnp.float32
        )
        d_scores = (probs * (probability_gradient - delta[..., None])).astype(jnp.bfloat16)
        return (probs, d_scores)

    def attend_back(step_idx, carry):
        d_query, d_keyval = carry
        block_kv = lax.dynamic_slice_in_dim(keyval_all, step_idx * key_block, key_block, 1)
        probs, d_scores = query_grad(block_kv, step_idx)
        d_query = d_query + jnp.einsum(
            "srhk,skd->srhd", d_scores, block_kv[..., :HEAD], preferred_element_type=jnp.float32
        )
        d_keys = (
            jnp.einsum("srhk,srhd->skd", d_scores, queries, preferred_element_type=jnp.float32)
            * scale
        )
        d_values = jnp.einsum(
            "srhk,srhd->skd", probs.astype(jnp.bfloat16), d_attn, preferred_element_type=jnp.float32
        )
        d_keyval = lax.dynamic_update_slice_in_dim(
            d_keyval, jnp.concatenate([d_keys, d_values], axis=-1), step_idx * key_block, 1
        )
        return (d_query, d_keyval)

    backward_initial_state = (
        jnp.zeros((seq_count, row_count, q_local, HEAD), jnp.float32),
        jnp.zeros((seq_count, seq_length, 2 * HEAD), jnp.float32),
    )
    d_query, d_keyval = lax.fori_loop(0, key_steps, attend_back, backward_initial_state)
    d_keyval_mine = lax.psum_scatter(
        d_keyval.astype(jnp.bfloat16), "ctx", scatter_dimension=1, tiled=True
    )
    d_query = (d_query * scale).astype(jnp.bfloat16).reshape(seq_count, row_count, q_local * HEAD)
    d_mixed_blocks = blocked(d_mixed, (heads_local, mamba_head))
    entry = (
        jnp.exp(log_decay) * (seg_blocks == seg_before[..., None]).astype(jnp.float32)[..., None]
    )
    local_grad = jnp.einsum(
        "abth,abthp,abtn->abhpn", entry, d_mixed_blocks, read_blocks, precision=exact_precision
    )
    first_back = (carried[:, 0], local_grad[:, 0])
    second_back = (carried[:, 1], local_grad[:, 1])
    climb = carried_in(second_back, "ctx", compose, identity, False)
    second_total = compose(climb, second_back)
    descend_in = choose(last_dev, compose(second_total, first_back), first_back)
    descend = carried_in(descend_in, "ctx", compose, identity, True)
    grad_end = jnp.stack([jnp.where(last_dev, second_total[1], descend[1]), climb[1]], axis=1)
    decay_cot = jnp.sum(grad_end * state_in, axis=(-2, -1))

    def whole(mix_vals, key_vals, read_vals, step_vals, rate_vals, skip_vals, state_vals):
        return over_blocks(block_scan, (0, 0, 0, 0, None, None, 0, 0, 0))(
            mix_vals,
            key_vals,
            read_vals,
            step_vals,
            rate_vals,
            skip_vals,
            seg_blocks,
            seg_before,
            state_vals,
        )

    _, backward_function = jax.vjp(
        whole, mix_blocks, key_blocks, read_blocks, step_blocks, decay_rate, skip_gain, state_in
    )
    grad_mix, grad_key, grad_read, grad_stepv, grad_rate, grad_skip, _ = backward_function(
        (d_mixed_blocks, decay_cot, grad_end)
    )
    d_mix_in = grad_mix.reshape(seq_count, row_count, heads_local * mamba_head).astype(jnp.bfloat16)
    d_key_vec = grad_key.reshape(seq_count, row_count, n_state).astype(jnp.bfloat16)
    d_read_vec = grad_read.reshape(seq_count, row_count, n_state).astype(jnp.bfloat16)
    d_step_raw = grad_stepv.reshape(seq_count, row_count, heads_local)
    grad_bias = jnp.sum(d_step_raw, axis=(0, 1))
    d_step_low = d_step_raw.astype(jnp.bfloat16)
    d_normed = lax.psum(
        (
            times_trans(d_query, query_weight)
            + times_trans(d_keyval_mine, keyval_mine)
            + times_trans(d_mix_in, mixin_weight)
            + times_trans(d_mix_gate, mixgate_weight)
            + times_trans(d_key_vec, inject_weight)
            + times_trans(d_read_vec, readout_weight)
            + times_trans(d_step_low, step_weight)
        ).astype(jnp.bfloat16),
        "tp",
    ).astype(jnp.float32)
    grad_first = jnp.sum(d_normed * hidden * first_scale, axis=(0, 1))
    grad_hidden = d_middle + norm_back(d_normed, first_gain, hidden, first_scale)
    grad_keyval = lax.dynamic_update_slice_in_dim(
        jnp.zeros(keyval_weight.shape, jnp.float32),
        outer_rows(normed, d_keyval_mine),
        kv_head * 2 * HEAD,
        1,
    )
    sharded = (
        lax.psum_scatter(
            outer_rows(normed, d_query).astype(jnp.bfloat16), "ctx", scatter_dimension=0, tiled=True
        ).astype(jnp.float32),
        lax.psum_scatter(
            grad_attn_out.astype(jnp.bfloat16), "ctx", scatter_dimension=1, tiled=True
        ).astype(jnp.float32),
        lax.psum_scatter(
            outer_rows(normed, d_mix_in).astype(jnp.bfloat16),
            "ctx",
            scatter_dimension=0,
            tiled=True,
        ).astype(jnp.float32),
        lax.psum_scatter(
            outer_rows(normed, d_mix_gate).astype(jnp.bfloat16),
            "ctx",
            scatter_dimension=0,
            tiled=True,
        ).astype(jnp.float32),
        lax.psum_scatter(
            outer_rows(normed, d_step_low).astype(jnp.bfloat16),
            "ctx",
            scatter_dimension=0,
            tiled=True,
        ).astype(jnp.float32),
        lax.psum_scatter(
            grad_mixout.astype(jnp.bfloat16), "ctx", scatter_dimension=1, tiled=True
        ).astype(jnp.float32),
        lax.psum_scatter(
            grad_gate.astype(jnp.bfloat16), "ctx", scatter_dimension=0, tiled=True
        ).astype(jnp.float32),
        lax.psum_scatter(
            grad_up.astype(jnp.bfloat16), "ctx", scatter_dimension=0, tiled=True
        ).astype(jnp.float32),
        lax.psum_scatter(
            grad_down.astype(jnp.bfloat16), "ctx", scatter_dimension=1, tiled=True
        ).astype(jnp.float32),
    )
    shared = (
        lax.psum_scatter(grad_keyval, ("ctx", "tp"), scatter_dimension=0, tiled=True),
        lax.psum_scatter(
            outer_rows(normed, d_key_vec), ("ctx", "tp"), scatter_dimension=0, tiled=True
        ),
        lax.psum_scatter(
            outer_rows(normed, d_read_vec), ("ctx", "tp"), scatter_dimension=0, tiled=True
        ),
    )
    small = lax.psum((grad_first, grad_second, grad_bias, grad_rate, grad_skip), "ctx")
    return (
        layer_out,
        grad_hidden,
        small[0],
        sharded[0],
        shared[0],
        sharded[1],
        sharded[2],
        sharded[3],
        shared[1],
        shared[2],
        sharded[4],
        small[2],
        small[3],
        small[4],
        sharded[5],
        small[1],
        sharded[6],
        sharded[7],
        sharded[8],
    )


def solution(mesh):
    placed = (
        P(None, "ctx", None),
        P(),
        P(),
        P(None, "tp"),
        P(),
        P("tp", None),
        P(None, "tp"),
        P(None, "tp"),
        P(),
        P(),
        P(None, "tp"),
        P("tp"),
        P("tp"),
        P("tp"),
        P("tp", None),
        P(),
        P(None, "tp"),
        P(None, "tp"),
        P("tp", None),
        P(None, "ctx", None),
    )
    return jax.shard_map(
        body,
        mesh=mesh,
        in_specs=placed,
        out_specs=(
            P(None, "ctx", None),
            P(None, "ctx", None),
            P(),
            P("ctx", "tp"),
            P(("ctx", "tp"), None),
            P("tp", "ctx"),
            P("ctx", "tp"),
            P("ctx", "tp"),
            P(("ctx", "tp"), None),
            P(("ctx", "tp"), None),
            P("ctx", "tp"),
            P("tp"),
            P("tp"),
            P("tp"),
            P("tp", "ctx"),
            P(),
            P("ctx", "tp"),
            P("ctx", "tp"),
            P("tp", "ctx"),
        ),
        check_vma=False,
    )
```

profile of v0, /device:TPU:0, one launch (start us, length us, event | category | flops | bytes accessed | tf_op | source)
XLA Modules:
  0.0 1459.3 jit_solution(6375244133129595669)
XLA Ops:
  33.3 5.4 gather_fusion
  42.6 22.5 %all-gather = bf16[16,1,6]{2,1,0:T(2,128)(2,1)S(1)} all-gather(bf16[2,1,6]{2,1,0:T(2,128)(2,1)} %get-tuple-element.1331), channel_id=2, replica_groups=mesh['ctx'=8,'tp'=4] {'ctx'}, dimensions={0}, use_global_device_ids=true | all-gather | bytes 216 | tf_op jit(solution)/shard_map/all_gather | solution.py:22
  74.1 19.3 %while.99 = (s32[]{:T(128)}, f32[2,6]{1,0:T(2,128)S(1)}, f32[2,6,64,128]{3,2,1,0:T(8,128)S(1)}, s32[]{:T(128)}, bf16[8,2,6]{2,1,0:T(2,128)(2,1)}, /*index=5*/bf16[8,2,6,64,128]{4,3,2,1,0:T(8,128)(2,1)}, s32[]{:T(128)}, s32[]{:T(128)}) while((s32[]{:T(128)}, f32[2,6]{1,0:T(2,128)S(1)}, f32[2,6,64,128]{3,2,1,0:T(8,128)S(1)}, ...), condition=%wide.region_7.8_spmd.clone, body=%wide.region_6.7_spmd.clone.sunk | while | flops 491584 | bytes 983407 | solution.py:40
  95.5 12.8 all-gather.16.cloned.1.call-done
  108.3 6.7 while.98
  118.2 18.5 %all-gather.8 = bf16[8,2,6]{2,1,0:T(2,128)(2,1)} all-gather(bf16[1,2,6]{2,1,0:T(2,128)(2,1)S(1)} %fusion.168), channel_id=4, replica_groups=mesh['ctx'=8,'tp'=4] {'ctx'}, dimensions={0}, use_global_device_ids=true | all-gather | bytes 216 | tf_op jit(solution)/shard_map/all_gather | solution.py:22
  136.7 17.3 %all-gather.20.cloned.1.call-done = bf16[16,6,64,128]{3,2,1,0:T(8,128)(2,1)} async-done(((bf16[2,6,64,128]{3,2,1,0:T(8,128)(2,1)}), bf16[16,6,64,128]{3,2,1,0:T(8,128)(2,1)}) %all-gather.20.cloned.1.call-update) | async-done | bytes 1572880 | tf_op jit(solution)/shard_map/all_gather | solution.py:22
  154.0 13.8 while.100
  179.4 31.8 %all-reduce.7.cloned.1.call-done = bf16[2,128,1024]{2,1,0:T(8,128)(2,1)} async-done(((bf16[2,128,1024]{2,1,0:T(8,128)(2,1)}), bf16[2,128,1024]{2,1,0:T(8,128)(2,1)}) %all-reduce.7.cloned.1.call-update) | async-done | bytes 524304 | tf_op jit(solution)/shard_map/psum | solution.py:275
  220.7 20.5 %all-gather.4 = bf16[16,1,6]{2,1,0:T(2,128)(2,1)S(1)} all-gather(bf16[2,1,6]{2,1,0:T(2,128)(2,1)S(1)} %copy-done.154), channel_id=6, replica_groups=mesh['ctx'=8,'tp'=4] {'ctx'}, dimensions={0}, use_global_device_ids=true | all-gather | bytes 216 | tf_op jit(solution)/shard_map/all_gather | solution.py:22
  242.3 10.9 all-reduce.9.cloned.1.call-done
  268.6 14.0 while.101
  286.4 25.2 %all-gather.22.cloned.1.call-done = bf16[16,1,6,64,128]{4,3,2,1,0:T(8,128)(2,1)} async-done(((bf16[2,1,6,64,128]{4,3,2,1,0:T(8,128)(2,1)}), bf16[16,1,6,64,128]{4,3,2,1,0:T(8,128)(2,1)}) %all-gather.22.cloned.1.call-update) | async-done | bytes 1572880 | tf_op jit(solution)/shard_map/all_gather | solution.py:22
  311.5 19.2 %while.102 = (s32[]{:T(128)}, f32[2,6]{1,0:T(2,128)S(1)}, f32[2,6,64,128]{3,2,1,0:T(8,128)S(1)}, s32[]{:T(128)}, bf16[8,2,6]{2,1,0:T(2,128)(2,1)}, /*index=5*/bf...) while((s32[]{:T(128)}, f32[2,6]{1,0:T(2,128)S(1)}, f32[2,6,64,128]{3,2,1,0:T(8,128)S(1)}, ...), condition=%wide.region_20.21_spmd.clone, body=%wide.region_19.20_spmd.clone.sunk | while | flops 491584 | bytes 983407 | solution.py:40
  349.1 11.4 reduce-scatter.36.cloned.1.call-start
  387.0 18.9 %all-gather.9 = bf16[8,2,6]{2,1,0:T(2,128)(2,1)} all-gather(bf16[1,2,6]{2,1,0:T(2,128)(2,1)S(1)} %fusion.167), channel_id=8, replica_groups=mesh['ctx'=8,'tp'=4] {'ctx'}, dimensions={0}, use_global_device_ids=true | all-gather | bytes 216 | tf_op jit(solution)/shard_map/all_gather | solution.py:22
  405.9 17.6 %all-gather.24.cloned.1.call-done = bf16[16,6,64,128]{3,2,1,0:T(8,128)(2,1)} async-done(((bf16[2,6,64,128]{3,2,1,0:T(8,128)(2,1)}), bf16[16,6,64,128]{3,2,1,0:T(8,128)(2,1)}) %all-gather.24.cloned.1.call-update) | async-done | bytes 1572880 | tf_op jit(solution)/shard_map/all_gather | solution.py:22
  423.5 13.7 while.103
  478.5 9.6 reduce-scatter.42.cloned.1.call-done
  489.7 62.5 %reduce-scatter.24.cloned.1.call-done = bf16[128,256]{1,0:T(8,128)(2,1)} async-done(((bf16[1024,256]{1,0:T(8,128)(2,1)}), bf16[128,256]{1,0:T(8,128)(2,1)}) %reduce-scatter.24.cloned.1.call-update) | async-done | bytes 65552 | tf_op jit(solution)/shard_map/reduce_scatter | solution.py:422
  553.7 63.6 %reduce-scatter.46.cloned.1.call-done = bf16[128,384]{1,0:T(8,128)(2,1)} async-done(((bf16[1024,384]{1,0:T(8,128)(2,1)}), bf16[128,384]{1,0:T(8,128)(2,1)}) %reduce-scatter.46.cloned.1.call-update) | async-done | bytes 98320
  619.1 62.9 %reduce-scatter.30.cloned.1.call-done = bf16[128,384]{1,0:T(8,128)(2,1)} async-done(((bf16[1024,384]{1,0:T(8,128)(2,1)}), bf16[128,384]{1,0:T(8,128)(2,1)}) %reduce-scatter.30.cloned.1.call-update) | async-done | bytes 98320 | tf_op jit(solution)/shard_map/reduce_scatter | solution.py:434
  683.6 64.7 %reduce-scatter.48.cloned.1.call-done = bf16[128,512]{1,0:T(8,128)(2,1)} async-done(((bf16[1024,512]{1,0:T(8,128)(2,1)}), bf16[128,512]{1,0:T(8,128)(2,1)}) %reduce-scatter.48.cloned.1.call-update) | async-done | bytes 131088
  750.1 63.9 %reduce-scatter.38.cloned.1.call-done = bf16[128,512]{1,0:T(8,128)(2,1)} async-done(((bf16[1024,512]{1,0:T(8,128)(2,1)}), bf16[128,512]{1,0:T(8,128)(2,1)}) %reduce-scatter.38.cloned.1.call-update) | async-done | bytes 131088 | tf_op jit(solution)/shard_map/reduce_scatter | solution.py:452
  815.7 64.5 %reduce-scatter.36.cloned.1.call-done = bf16[128,512]{1,0:T(8,128)(2,1)} async-done(((bf16[1024,512]{1,0:T(8,128)(2,1)}), bf16[128,512]{1,0:T(8,128)(2,1)}) %reduce-scatter.36.cloned.1.call-update) | async-done | bytes 131088 | tf_op jit(solution)/shard_map/reduce_scatter | solution.py:449
  882.0 61.6 %reduce-scatter.44.cloned.1.call-done = bf16[128,6]{1,0:T(8,128)(2,1)} async-done(((bf16[1024,6]{1,0:T(8,128)(2,1)}), bf16[128,6]{1,0:T(8,128)(2,1)}) %reduce-scatter.44.cloned.1.call-update) | async-done | bytes 1552
  945.0 36.7 %all-reduce.11.cloned.1.call-done = (bf16[2,128,1024]{2,1,0:T(8,128)(2,1)}, bf16[2,128,1024]{2,1,0:T(8,128)(2,1)}) async-done(((bf16[2,128,1024]{2,1,0:T(8,128)(2,1)}, bf16[2,128,1024]{2,1,0:T(8,128)(2,1)}), (bf16[2,128,1024]{2,1,0:T(8,128)(2,1)}, bf16[2,128,1024]{2,1,0:T(8,128)(2,1)})) %all-reduce.11.cloned.1.call-update) | async-done | bytes 1048592 | tf_op jit(solution)/shard_map/psum | solution.py:289
  983.2 22.7 %all-reduce.1 = (f32[1024]{0:T(1024)}, f32[6]{0:T(128)}, f32[6]{0:T(128)}, f32[6]{0:T(128)}, f32[1024]{0:T(1024)}) all-reduce(f32[1024]{0:T(1024)S(1)} %get-tuple-element.1195, f32[6]{0:T(128)S(1)} %copy-done.158, f32[6]{0:T(128)S(1)} %neg.45, f32[6]{0:T(128)S(1)} %reduce_sum.241, ...), channel_id=1, replica_groups=mesh['ctx'=8,'tp'=4] {'ctx'}, use_global_device_ids=true, to_apply=%region_34.35 | all-reduce | flops 2066 | bytes 16528 | tf_op jit(solution)/shard_map/psum | solution.py:468
  1009.0 39.2 %reduce-scatter.28.cloned.1.call-done = bf16[128,384]{1,0:T(8,128)(2,1)} async-done(((bf16[1024,384]{1,0:T(8,128)(2,1)}), bf16[128,384]{1,0:T(8,128)(2,1)}) %reduce-scatter.28.cloned.1.call-update) | async-done | bytes 98320 | tf_op jit(solution)/shard_map/reduce_scatter | solution.py:428
  1049.8 134.0 %reduce-scatter.34.cloned.1.call-done = f32[32,128]{1,0:T(8,128)} async-done(((f32[1024,128]{1,0:T(8,128)}), f32[32,128]{1,0:T(8,128)}) %reduce-scatter.34.cloned.1.call-update) | async-done | bytes 16400 | tf_op jit(solution)/shard_map/reduce_scatter | solution.py:464
  1183.8 135.6 %reduce-scatter.26.cloned.1.call-done = f32[32,512]{1,0:T(8,128)} async-done(((f32[1024,512]{1,0:T(8,128)}), f32[32,512]{1,0:T(8,128)}) %reduce-scatter.26.cloned.1.call-update) | async-done | bytes 65552 | tf_op jit(solution)/shard_map/reduce_scatter | solution.py:460
  1319.3 132.9 %reduce-scatter.32.cloned.1.call-done = f32[32,128]{1,0:T(8,128)} async-done(((f32[1024,128]{1,0:T(8,128)}), f32[32,128]{1,0:T(8,128)}) %reduce-scatter.32.cloned.1.call-update) | async-done | bytes 16400 | tf_op jit(solution)/shard_map/reduce_scatter | solution.py:461
  (694 shorter events, 274.6 us)
Async XLA Ops:
  7.3 66.9 %all-gather.18.cloned.1.call-start = ((), (), s32[]{:S(2)}) async-start(), calls=%async_computation.24 | async-start | bytes 1769472 | tf_op jit(solution)/shard_map/all_gather | solution.py:22
  19.4 88.9 %all-gather.16.cloned.1.call-start = ((), (), s32[]{:S(2)}) async-start(), calls=%async_computation.13 | async-start | bytes 1179648 | tf_op jit(solution)/shard_map/all_gather | solution.py:179
  21.5 132.5 %all-gather.20.cloned.1.call-start = ((), (), s32[]{:S(2)}) async-start(), calls=%async_computation.25 | async-start | bytes 1769472 | tf_op jit(solution)/shard_map/all_gather | solution.py:22
  95.4 115.8 %all-reduce.7.cloned.1.call-start = ((), (), s32[]{:S(2)}) async-start(), calls=%async_computation.14 | async-start | bytes 1048576 | tf_op jit(solution)/shard_map/psum | solution.py:275
  179.1 74.1 %all-reduce.9.cloned.1.call-start = ((), (), s32[]{:S(2)}) async-start(), calls=%async_computation.15 | async-start | bytes 1048576 | tf_op jit(solution)/shard_map/psum | solution.py:301
  219.8 91.7 %all-gather.22.cloned.1.call-start = ((), (), s32[]{:S(2)}) async-start(), calls=%async_computation.26 | async-start | bytes 1769472 | tf_op jit(solution)/shard_map/all_gather | solution.py:22
  267.4 113.5 %reduce-scatter.40.cloned.1.call-start = ((), (), s32[]{:S(2)}) async-start(), calls=%async_computation.28 | async-start | bytes 1179648
  286.3 137.2 %all-gather.24.cloned.1.call-start = ((), (), s32[]{:S(2)}) async-start(), calls=%async_computation.27 | async-start | bytes 1769472 | tf_op jit(solution)/shard_map/all_gather | solution.py:22
  332.9 155.2 %reduce-scatter.42.cloned.1.call-start = ((), (), s32[]{:S(2)}) async-start(), calls=%async_computation.29 | async-start | bytes 589824
  336.2 216.1 %reduce-scatter.24.cloned.1.call-start = ((), (), s32[]{:S(2)}) async-start(), calls=%async_computation.16 | async-start | bytes 589824 | tf_op jit(solution)/shard_map/reduce_scatter | solution.py:422
  338.4 279.0 %reduce-scatter.46.cloned.1.call-start = ((), (), s32[]{:S(2)}) async-start(), calls=%async_computation.31 | async-start | bytes 884736
  342.0 340.0 %reduce-scatter.30.cloned.1.call-start = ((), (), s32[]{:S(2)}) async-start(), calls=%async_computation.19 | async-start | bytes 884736 | tf_op jit(solution)/shard_map/reduce_scatter | solution.py:434
  343.6 404.8 %reduce-scatter.48.cloned.1.call-start = ((), (), s32[]{:S(2)}) async-start(), calls=%async_computation.32 | async-start | bytes 1179648
  347.5 466.5 %reduce-scatter.38.cloned.1.call-start = ((), (), s32[]{:S(2)}) async-start(), calls=%async_computation.23 | async-start | bytes 1179648 | tf_op jit(solution)/shard_map/reduce_scatter | solution.py:452
  349.1 531.1 %reduce-scatter.36.cloned.1.call-start = ((), (), s32[]{:S(2)}) async-start(), calls=%async_computation.22 | async-start | bytes 1179648 | tf_op jit(solution)/shard_map/reduce_scatter | solution.py:449
  364.1 579.5 %reduce-scatter.44.cloned.1.call-start = ((), (), s32[]{:S(2)}) async-start(), calls=%async_computation.30 | async-start | bytes 294912
  466.4 515.4 %all-reduce.11.cloned.1.call-start = ((), (), s32[]{:S(2)}) async-start(), calls=%async_computation.33 | async-start | bytes 2097152 | tf_op jit(solution)/shard_map/psum | solution.py:289
  470.6 577.5 %reduce-scatter.28.cloned.1.call-start = ((), (), s32[]{:S(2)}) async-start(), calls=%async_computation.18 | async-start | bytes 884736 | tf_op jit(solution)/shard_map/reduce_scatter | solution.py:428
  472.2 711.6 %reduce-scatter.34.cloned.1.call-start = ((), (), s32[]{:S(2)}) async-start(), calls=%async_computation.21 | async-start | bytes 540672 | tf_op jit(solution)/shard_map/reduce_scatter | solution.py:464
  473.5 845.8 %reduce-scatter.26.cloned.1.call-start = ((), (), s32[]{:S(2)}) async-start(), calls=%async_computation.17 | async-start | bytes 2162688 | tf_op jit(solution)/shard_map/reduce_scatter | solution.py:460
  476.7 975.5 %reduce-scatter.32.cloned.1.call-start = ((), (), s32[]{:S(2)}) async-start(), calls=%async_computation.20 | async-start | bytes 540672 | tf_op jit(solution)/shard_map/reduce_scatter | solution.py:461
  478.3 403.6 %copy-start.135 = (f32[2,128,6]{1,2,0:T(8,128)S(1)}, f32[2,128,6]{1,2,0:T(8,128)}, u32[]{:S(2)}) copy-start(f32[2,128,6]{1,2,0:T(8,128)} %copy-done.134) | copy-start | bytes 18436
  478.3 403.6 %copy-start.159 = (u8[128,6]{0,1:T(8,128)(4,1)S(1)}, u8[128,6]{0,1:T(8,128)(4,1)}, u32[]{:S(2)}) copy-start(u8[128,6]{0,1:T(8,128)(4,1)} %get-tuple-element.1340) | copy-start | bytes 2308
  619.1 364.1 %copy-start.158 = (f32[6]{0:T(128)S(1)}, f32[6]{0:T(128)}, u32[]{:S(2)}) copy-start(f32[6]{0:T(128)} %get-tuple-element.1304) | copy-start | bytes 76
  619.1 386.8 %copy-start.4 = (bf16[2,128,1024]{2,1,0:T(8,128)(2,1)S(1)}, bf16[2,128,1024]{2,1,0:T(8,128)(2,1)}, u32[]{:S(2)}) copy-start(bf16[2,128,1024]{2,1,0:T(8,128)(2,1)} %all-reduce.7.cloned.1.call-done) | copy-start | bytes 1572868
  619.1 386.8 %copy-start.28 = (bf16[2,128,1024]{2,1,0:T(8,128)(2,1)S(1)}, bf16[2,128,1024]{2,1,0:T(8,128)(2,1)}, u32[]{:S(2)}) copy-start(bf16[2,128,1024]{2,1,0:T(8,128)(2,1)} %param.51) | copy-start | bytes 1572868
  619.1 386.8 %copy-start.30 = (bf16[2,128,1024]{2,1,0:T(8,128)(2,1)S(1)}, bf16[2,128,1024]{2,1,0:T(8,128)(2,1)}, u32[]{:S(2)}) copy-start(bf16[2,128,1024]{2,1,0:T(8,128)(2,1)} %all-reduce.9.cloned.1.call-done) | copy-start | bytes 1572868
  619.1 386.8 %copy-start.117 = (f32[1024]{0:T(1024)S(1)}, f32[1024]{0:T(1024)}, u32[]{:S(2)}) copy-start(f32[1024]{0:T(1024)} %param.47) | copy-start | bytes 12292
  619.1 386.8 %copy-start.137 = (f32[2,128]{1,0:T(2,128)S(1)}, f32[2,128]{1,0:T(2,128)}, u32[]{:S(2)}) copy-start(f32[2,128]{1,0:T(2,128)} %copy-done.136) | copy-start | bytes 3076
  619.1 386.8 %copy-start.146 = (f32[2,128]{1,0:T(2,128)S(1)}, f32[2,128]{1,0:T(2,128)}, u32[]{:S(2)}) copy-start(f32[2,128]{1,0:T(2,128)} %copy-done.145) | copy-start | bytes 3076
  619.1 386.8 %copy-start.148 = (f32[2,128]{1,0:T(2,128)S(1)}, f32[2,128]{1,0:T(2,128)}, u32[]{:S(2)}) copy-start(f32[2,128]{1,0:T(2,128)} %copy-done.147) | copy-start | bytes 3076
  619.1 386.8 %copy-start.153 = (f32[2,128]{1,0:T(2,128)S(1)}, f32[2,128]{1,0:T(2,128)}, u32[]{:S(2)}) copy-start(f32[2,128]{1,0:T(2,128)} %get-tuple-element.1334) | copy-start | bytes 3076
  (156 other events, 1795.7 us)
Sparse Core Ops, SparseCore 0:
  19.5 46.9 all-gather.17
  69.3 38.9 all-gather.15
  111.0 42.9 all-gather.19
  179.2 31.9 all-reduce.6
  220.0 33.1 all-reduce.8
  267.5 43.9 all-gather.21
  314.9 62.2 reduce-scatter.39
  380.3 43.2 all-gather.23
  427.2 60.7 reduce-scatter.41
  491.3 60.9 reduce-scatter.23
  555.9 61.3 reduce-scatter.45
  620.5 61.5 reduce-scatter.29
  685.8 62.4 reduce-scatter.47
  751.6 62.3 reduce-scatter.37
  817.7 62.4 reduce-scatter.35
  883.3 60.2 reduce-scatter.43
  946.5 35.2 all-reduce.10
  985.3 62.8 reduce-scatter.27
  1051.0 132.7 reduce-scatter.33
  1186.5 132.7 reduce-scatter.25
  1322.1 130.0 reduce-scatter.31
where the time goes:
time: 1470 us; the launch traced here: 1460 us
  waiting for transfers between devices  1050 us (71%)
  other arithmetic  123 us (8%)
  blocking collectives  103 us (7%)
  matrix products  78.6 us (5%)
  local copies, waits for them, and re-layouts  77 us (5%)
  between operations  16.4 us (1%)
    unnamed x26, waiting for transfers between devices  200 us
    reduce_scatter x1, waiting for transfers between devices, body(): lax.psum_scatter(grad_keyval, ('ctx', 'tp'), scatter_dimension=0, tiled=T...  136 us
    reduce_scatter x1, waiting for transfers between devices, body(): lax.psum_scatter(outer_rows(normed, d_read_vec), ('ctx', 'tp'), scatter_d...  134 us
    reduce_scatter x1, waiting for transfers between devices, body(): lax.psum_scatter(outer_rows(normed, d_key_vec), ('ctx', 'tp'), scatter_di...  133 us
    all_gather x4, blocking collectives, carried_in(): lax.all_gather(part.astype(kind), axis)  80.3 us
    reduce_scatter x1, waiting for transfers between devices, body(): lax.psum_scatter(grad_gate.astype(jnp.bfloat16), 'ctx', scatter_dimension...  64.5 us
    reduce_scatter x1, waiting for transfers between devices, body(): lax.psum_scatter(grad_up.astype(jnp.bfloat16), 'ctx', scatter_dimension=0...  63.9 us
    reduce_scatter x1, waiting for transfers between devices, body(): lax.psum_scatter(outer_rows(normed, d_mix_gate).astype(jnp.bfloat16), 'ct...  62.9 us
  transfers between devices with their start and end apart: 21, of which 19 were waited for; matrix products, arithmetic and copies ran while one was open for 15% of the time, Pallas kernels for 0%

commit v1 on v0

v1 whole, which is shorter than its diff:
```python
import jax
import jax.numpy as jnp
from jax import lax
from jax.sharding import PartitionSpec as P

QHEADS = 8
KVHEADS = 2
HEAD = 128


NORM_EPS = 1e-05
MASK_FILL = -1e30
FAR_BELOW = -10000.0
exact_precision = lax.Precision.HIGHEST


def spread(array, axes):
    return lax.all_to_all(array, axes, 0, 0, tiled=True)


def row_chunks(array, count):
    return array.reshape((count, array.shape[0] // count) + array.shape[1:])


def three_parts(value):
    high = lax.reduce_precision(value, 8, 7)
    rest = value - high
    mid = lax.reduce_precision(rest, 8, 7)
    return jnp.stack([high, mid, rest - mid]).astype(jnp.bfloat16)


def decays(step_raw, decay_rate):
    step_size = jax.nn.softplus(step_raw)
    return (step_size, jnp.cumsum(-decay_rate[None, :] * step_size, axis=0))


def state_part(mix_in, key_vec, step_size, log_decay, seg_here, seg_before):
    log_end = log_decay[-1]
    same_end = (seg_here == seg_here[-1]).astype(jnp.float32)
    end_weight = jnp.exp(log_end[None, :] - log_decay) * same_end[:, None] * step_size
    state = jnp.einsum("sh,shp,sn->hpn", end_weight, mix_in, key_vec, precision=exact_precision)
    carried = jnp.exp(log_end) * (seg_here[-1] == seg_before).astype(jnp.float32)
    return (carried, state)


def out_part(
    mix_in, key_vec, read_vec, step_size, log_decay, skip_gain, seg_here, seg_before, state_in
):
    places = jnp.arange(seg_here.shape[0], dtype=jnp.int32)
    visible = (places[:, None] >= places[None, :]) & (seg_here[:, None] == seg_here[None, :])
    log_gap = log_decay[:, None, :] - log_decay[None, :, :]
    weights = jnp.exp(jnp.where(visible[:, :, None], log_gap, FAR_BELOW)) * step_size[None, :, :]
    mixing = jnp.einsum("tn,sn->ts", read_vec, key_vec, precision=exact_precision)
    result = jnp.einsum(
        "tsh,shp->thp", weights * mixing[:, :, None], mix_in, precision=exact_precision
    )
    entry = jnp.exp(log_decay) * (seg_here == seg_before).astype(jnp.float32)[:, None]
    result = result + entry[:, :, None] * jnp.einsum(
        "tn,hpn->thp", read_vec, state_in, precision=exact_precision
    )
    return result + skip_gain[None, :, None] * mix_in


def block_scan(
    mix_in, key_vec, read_vec, step_raw, decay_rate, skip_gain, seg_here, seg_before, state_in
):
    step_size, log_decay = decays(step_raw, decay_rate)
    carried, state = state_part(mix_in, key_vec, step_size, log_decay, seg_here, seg_before)
    result = out_part(
        mix_in, key_vec, read_vec, step_size, log_decay, skip_gain, seg_here, seg_before, state_in
    )
    return (result, carried, state)


def over_blocks(function, axes):
    return jax.vmap(jax.vmap(function, in_axes=axes), in_axes=axes)


def rms_scale(value_rows):
    return lax.rsqrt(jnp.mean(value_rows * value_rows, axis=-1, keepdims=True) + NORM_EPS)


def norm_back(d_norm, gain, value_rows, scale):
    d_hat = d_norm * gain
    return scale * d_hat - value_rows * scale**3 * jnp.mean(
        d_hat * value_rows, axis=-1, keepdims=True
    )


def times_trans(grad, weight_matrix):
    return lax.dot_general(
        grad,
        weight_matrix,
        (((grad.ndim - 1,), (1,)), ((), ())),
        preferred_element_type=jnp.float32,
    )


def outer_rows(left, right):
    return lax.dot_general(
        left, right, (((0,), (0,)), ((), ())), preferred_element_type=jnp.float32
    )


def body(
    hidden_in,
    seg_ids,
    first_gain,
    query_weight,
    keyval_weight,
    attn_out_weight,
    mixin_weight,
    mixgate_weight,
    inject_weight,
    readout_weight,
    step_weight,
    step_bias,
    decay_rate,
    skip_gain,
    mixout_weight,
    second_gain,
    gate_weight,
    up_weight,
    down_weight,
    cotangent,
):
    ctx_size = lax.axis_size("ctx")
    tp_size = lax.axis_size("tp")
    ctx_index = lax.axis_index("ctx")
    tp_index = lax.axis_index("tp")
    seq_count, row_count, width = hidden_in.shape
    block_rows = row_count // 2
    block_count = 2 * ctx_size
    q_local = query_weight.shape[1] // HEAD
    heads_local = step_weight.shape[1]
    inner_local = mixin_weight.shape[1]
    mamba_head = inner_local // heads_local
    n_state = inject_weight.shape[1]
    ff_local = gate_weight.shape[1]
    kv_head = tp_index * q_local // (QHEADS // KVHEADS)
    scale = HEAD ** (-0.5)
    all_rows = seq_count * row_count

    local_rows = jnp.arange(row_count, dtype=jnp.int32)
    devices = jnp.arange(ctx_size, dtype=jnp.int32)

    def positions(device, local):
        return jnp.where(
            local < block_rows,
            device * block_rows + local,
            (block_count - 1 - device) * block_rows + local - block_rows,
        )

    q_places = positions(ctx_index, local_rows)
    k_places = positions(devices[:, None], local_rows[None, :]).reshape(-1)
    seg_by_block = seg_ids.reshape(seq_count, block_count, block_rows)
    k_segs = jnp.concatenate(
        [seg_by_block[:, :ctx_size], seg_by_block[:, ctx_size:][:, ::-1]], axis=2
    ).reshape(seq_count, ctx_size * row_count)
    q_segs = lax.dynamic_slice_in_dim(k_segs, ctx_index * row_count, row_count, 1)
    seg_end = seg_by_block[:, :, -1]
    own_blocks = jnp.stack([ctx_index, block_count - 1 - ctx_index])
    block_ids = jnp.arange(block_count, dtype=jnp.int32)
    is_before = block_ids[None, :] == own_blocks[:, None] - 1
    seg_before = jnp.sum(
        jnp.where(is_before[None], seg_end[:, None, :], 0), axis=-1
    ) - jnp.where(own_blocks == 0, 1, 0)

    step_pad = -heads_local % 128
    step_cols = heads_local + step_pad
    keyval_mine = lax.dynamic_slice_in_dim(keyval_weight, kv_head * 2 * HEAD, 2 * HEAD, 1)
    step_wide = jnp.pad(step_weight, ((0, 0), (0, step_pad)))
    weights_in = jnp.concatenate(
        [
            query_weight,
            mixin_weight,
            step_wide,
            mixgate_weight,
            keyval_mine,
            inject_weight,
            readout_weight,
        ],
        axis=1,
    )
    sizes_in = (
        q_local * HEAD,
        inner_local,
        step_cols,
        inner_local,
        2 * HEAD,
        n_state,
        n_state,
    )
    bounds = []
    at = 0
    for size in sizes_in:
        at += size
        bounds.append(at)

    hidden = hidden_in.astype(jnp.float32).reshape(all_rows, width)
    cotan = cotangent.reshape(all_rows, width)
    first_scale = rms_scale(hidden)
    normed = (hidden * first_scale * first_gain).astype(jnp.bfloat16)
    projected = jnp.dot(normed, weights_in, preferred_element_type=jnp.float32)
    queries, mix_in, step_raw, mix_gate, keyval, key_vec, read_vec = jnp.split(
        projected, bounds[:-1], axis=1
    )
    queries = queries.astype(jnp.bfloat16).reshape(seq_count, row_count, q_local, HEAD)
    keyval = keyval.astype(jnp.bfloat16).reshape(seq_count, row_count, 2 * HEAD)
    mix_in = mix_in.astype(jnp.bfloat16)
    key_vec = key_vec.astype(jnp.bfloat16)
    read_vec = read_vec.astype(jnp.bfloat16)
    step_raw = step_raw[:, :heads_local] + step_bias

    def blocked(value_rows, tail):
        return value_rows.reshape((seq_count, 2, block_rows) + tail)

    mix_blocks = blocked(mix_in.astype(jnp.float32), (heads_local, mamba_head))
    key_blocks = blocked(key_vec.astype(jnp.float32), (n_state,))
    read_blocks = blocked(read_vec.astype(jnp.float32), (n_state,))
    step_blocks = blocked(step_raw, (heads_local,))
    seg_blocks = blocked(q_segs, ())
    step_size, log_decay = over_blocks(decays, (0, None))(step_blocks, decay_rate)

    log_end = log_decay[:, :, -1, :].reshape(seq_count, 2 * heads_local)
    parts = jnp.moveaxis(three_parts(log_end), 0, 1).reshape(seq_count, 1, 6 * heads_local)
    extra_rows = jnp.pad(parts, ((0, 0), (0, 15), (0, 2 * HEAD - 6 * heads_local)))
    gathered = lax.all_gather(jnp.concatenate([keyval, extra_rows], axis=1), "ctx")
    keyval_all = jnp.swapaxes(gathered[:, :, :row_count], 0, 1).reshape(
        seq_count, ctx_size * row_count, 2 * HEAD
    )
    keys_all, values_all = keyval_all[..., :HEAD], keyval_all[..., HEAD:]
    decay_all = jnp.sum(
        gathered[:, :, row_count, : 6 * heads_local]
        .astype(jnp.float32)
        .reshape(ctx_size, seq_count, 3, 2, heads_local),
        axis=2,
    )
    log_blocks = jnp.concatenate([decay_all[:, :, 0], decay_all[::-1, :, 1]], axis=0)
    log_sum = jnp.cumsum(log_blocks, axis=0)

    log_prev = jnp.concatenate([jnp.zeros_like(log_sum[:1]), log_sum[:-1]], axis=0)
    seg_end_t = seg_end.T
    seg_prev_t = jnp.concatenate([jnp.full_like(seg_end_t[:1], -1), seg_end_t[:-1]], axis=0)

    def picked(table):
        return jnp.stack(
            [
                lax.dynamic_index_in_dim(table, own_blocks[0], 0, keepdims=False),
                lax.dynamic_index_in_dim(table, own_blocks[1], 0, keepdims=False),
            ]
        )

    def block_weights(valid, gap):
        weight = jnp.exp(jnp.where(valid[..., None], gap, FAR_BELOW))
        weight = jnp.where(valid[..., None], weight, 0.0)
        halves = jnp.stack([weight[:, :ctx_size], weight[:, ctx_size:][:, ::-1]], axis=2)
        return halves

    order = block_ids[None, :, None]
    own = own_blocks[:, None, None]
    rise = block_weights(
        (order < own) & (seg_end_t[None] == picked(seg_prev_t)[:, None]),
        picked(log_prev)[:, None] - log_sum[None],
    )
    fall = block_weights(
        (order > own) & (seg_prev_t[None] == picked(seg_end_t)[:, None]),
        log_prev[None] - picked(log_sum)[:, None],
    )

    def weighted(weight, blocks):
        total = 0.0
        for half in range(2):
            total = total + jnp.sum(
                weight[:, :, half][..., None, None]
                * blocks[None, :, :, half].astype(jnp.float32),
                axis=1,
            )
        return jnp.swapaxes(total, 0, 1)

    carried, state = over_blocks(state_part, (0, 0, 0, 0, 0, 0))(
        mix_blocks, key_blocks, step_size, log_decay, seg_blocks, seg_before
    )
    state_all = lax.all_gather(state.astype(jnp.bfloat16), "ctx")

    scores = (
        jnp.einsum("srhd,skd->srhk", queries, keys_all, preferred_element_type=jnp.float32) * scale
    )
    visible = (k_places[None, None, :] <= q_places[None, :, None]) & (
        k_segs[:, None, :] == q_segs[:, :, None]
    )
    scores = jnp.where(visible[:, :, None, :], scores, MASK_FILL)
    top = jnp.max(scores, axis=-1, keepdims=True)
    raised = jnp.exp(scores - top)
    probs = raised / jnp.sum(raised, axis=-1, keepdims=True)
    probs_low = probs.astype(jnp.bfloat16)
    attn_full = jnp.einsum(
        "srhk,skd->srhd", probs_low, values_all, preferred_element_type=jnp.float32
    )
    attn_low = attn_full.astype(jnp.bfloat16).reshape(all_rows, q_local * HEAD)

    state_in = weighted(rise, state_all)
    mixed = over_blocks(out_part, (0, 0, 0, 0, 0, None, 0, 0, 0))(
        mix_blocks,
        key_blocks,
        read_blocks,
        step_size,
        log_decay,
        skip_gain,
        seg_blocks,
        seg_before,
        state_in,
    )
    mixed = mixed.reshape(all_rows, inner_local)
    mixgate_sig = jax.nn.sigmoid(mix_gate)
    gate_act = mix_gate * mixgate_sig
    gated = (mixed * gate_act).astype(jnp.bfloat16)
    branch_in = jnp.concatenate([attn_low, gated], axis=1)
    weights_out = jnp.concatenate([attn_out_weight, mixout_weight], axis=0)
    branch = lax.psum(
        jnp.dot(branch_in, weights_out, preferred_element_type=jnp.float32).astype(jnp.bfloat16),
        "tp",
    ).astype(jnp.float32)
    middle = hidden + branch
    second_scale = rms_scale(middle)
    normed_two = (middle * second_scale * second_gain).astype(jnp.bfloat16)
    weights_ff = jnp.concatenate([gate_weight, up_weight], axis=1)
    gate_up = jnp.dot(normed_two, weights_ff, preferred_element_type=jnp.float32)
    gate, up_val = gate_up[:, :ff_local], gate_up[:, ff_local:]
    gate_sig = jax.nn.sigmoid(gate)
    inner = (gate * gate_sig * up_val).astype(jnp.bfloat16)
    inner_gradient = times_trans(cotan, down_weight)
    d_gate = (inner_gradient * up_val * gate_sig * (1.0 + gate * (1.0 - gate_sig))).astype(
        jnp.bfloat16
    )
    d_up = (inner_gradient * gate * gate_sig).astype(jnp.bfloat16)
    d_gate_up = jnp.concatenate([d_gate, d_up], axis=1)
    second_normed_gradient = lax.psum(
        times_trans(d_gate_up, weights_ff).astype(jnp.bfloat16), "tp"
    ).astype(jnp.float32)
    mlp_out = lax.psum(
        jnp.dot(inner, down_weight, preferred_element_type=jnp.float32).astype(jnp.bfloat16), "tp"
    )

    def outer_low(left, right):
        return outer_rows(left, right).astype(jnp.bfloat16)

    ff_grads = spread(
        row_chunks(
            jnp.concatenate([outer_low(normed_two, d_gate_up), outer_low(cotan, inner)], axis=1),
            ctx_size,
        ),
        "ctx",
    )

    grad_second = jnp.sum(second_normed_gradient * middle * second_scale, axis=0)
    d_middle = cotan.astype(jnp.float32) + norm_back(
        second_normed_gradient, second_gain, middle, second_scale
    )
    d_branch = d_middle.astype(jnp.bfloat16)
    d_branch_in = times_trans(d_branch, weights_out).astype(jnp.bfloat16)
    d_attn = d_branch_in[:, : q_local * HEAD].reshape(seq_count, row_count, q_local, HEAD)
    d_gated = d_branch_in[:, q_local * HEAD :].astype(jnp.float32)
    d_mixed = d_gated * gate_act
    d_mix_gate = (d_gated * mixed * mixgate_sig * (1.0 + mix_gate * (1.0 - mixgate_sig))).astype(
        jnp.bfloat16
    )

    d_mixed_blocks = blocked(d_mixed, (heads_local, mamba_head))
    entry = (
        jnp.exp(log_decay) * (seg_blocks == seg_before[..., None]).astype(jnp.float32)[..., None]
    )
    local_grad = jnp.einsum(
        "abth,abthp,abtn->abhpn", entry, d_mixed_blocks, read_blocks, precision=exact_precision
    )
    grad_all = lax.all_gather(local_grad.astype(jnp.bfloat16), "ctx")

    delta = jnp.sum(d_attn.astype(jnp.float32) * attn_full, axis=-1, keepdims=True)
    d_probs = jnp.einsum("srhd,skd->srhk", d_attn, values_all, preferred_element_type=jnp.float32)
    d_scores = (probs * (d_probs - delta)).astype(jnp.bfloat16)
    d_keys = (
        jnp.einsum("srhk,srhd->skd", d_scores, queries, preferred_element_type=jnp.float32) * scale
    ).astype(jnp.bfloat16)
    d_values = jnp.einsum(
        "srhk,srhd->skd", probs_low, d_attn, preferred_element_type=jnp.float32
    ).astype(jnp.bfloat16)
    d_keyval = jnp.concatenate([d_keys, d_values], axis=-1).reshape(
        seq_count, ctx_size, row_count, 2 * HEAD
    )
    d_keyval = spread(jnp.swapaxes(d_keyval, 0, 1), "ctx")
    d_query = (
        jnp.einsum("srhk,skd->srhd", d_scores, keys_all, preferred_element_type=jnp.float32) * scale
    )
    d_query = d_query.astype(jnp.bfloat16).reshape(all_rows, q_local * HEAD)
    out_grads = spread(
        row_chunks(
            jnp.concatenate([outer_low(d_branch, branch_in), outer_low(normed, d_mix_gate)], axis=1),
            ctx_size,
        ),
        "ctx",
    )
    d_keyval = jnp.sum(d_keyval.astype(jnp.float32), axis=0).astype(jnp.bfloat16)
    d_keyval = d_keyval.reshape(all_rows, 2 * HEAD)

    grad_end = weighted(fall, grad_all)
    decay_cot = jnp.sum(grad_end * state_in, axis=(-2, -1))

    def whole(mix_vals, key_vals, read_vals, step_vals, rate_vals, skip_vals, state_vals):
        return over_blocks(block_scan, (0, 0, 0, 0, None, None, 0, 0, 0))(
            mix_vals,
            key_vals,
            read_vals,
            step_vals,
            rate_vals,
            skip_vals,
            seg_blocks,
            seg_before,
            state_vals,
        )

    _, backward_function = jax.vjp(
        whole, mix_blocks, key_blocks, read_blocks, step_blocks, decay_rate, skip_gain, state_in
    )
    grad_mix, grad_key, grad_read, grad_stepv, grad_rate, grad_skip, _ = backward_function(
        (d_mixed_blocks, decay_cot, grad_end)
    )
    d_mix_in = grad_mix.reshape(all_rows, inner_local).astype(jnp.bfloat16)
    d_key_vec = grad_key.reshape(all_rows, n_state).astype(jnp.bfloat16)
    d_read_vec = grad_read.reshape(all_rows, n_state).astype(jnp.bfloat16)
    d_step_raw = grad_stepv.reshape(all_rows, heads_local)
    grad_bias = jnp.sum(d_step_raw, axis=0)
    d_step_wide = jnp.pad(d_step_raw.astype(jnp.bfloat16), ((0, 0), (0, step_pad)))
    d_unsplit = jnp.concatenate([d_keyval, d_key_vec, d_read_vec], axis=1)
    d_split = jnp.concatenate([d_query, d_mix_in, d_step_wide], axis=1)
    d_projected = jnp.concatenate([d_split, d_mix_gate, d_unsplit], axis=1)
    d_projected, mlp_out = lax.optimization_barrier((d_projected, mlp_out))
    layer_out = (middle + mlp_out.astype(jnp.float32)).astype(jnp.bfloat16)
    d_normed_part = times_trans(d_projected, weights_in)
    first_part = jnp.sum(d_normed_part * hidden * first_scale, axis=0)
    d_normed = lax.psum(d_normed_part.astype(jnp.bfloat16), "tp").astype(jnp.float32)
    in_grads = spread(row_chunks(outer_low(normed, d_split), ctx_size), "ctx")
    unsplit_grads = spread(
        row_chunks(outer_low(normed, d_unsplit), ctx_size * tp_size), ("ctx", "tp")
    )

    per_head = jnp.stack([grad_bias, grad_rate, grad_skip])
    slots = jnp.where(
        (jnp.arange(tp_size, dtype=jnp.int32) == tp_index)[:, None, None], per_head[None], 0.0
    )
    small = lax.psum(
        jnp.concatenate(
            [first_part, jnp.where(tp_index == 0, grad_second, 0.0), slots.reshape(-1)]
        ),
        ("ctx", "tp"),
    )
    head_sums = lax.dynamic_index_in_dim(
        small[2 * width :].reshape(tp_size, 3, heads_local), tp_index, 0, keepdims=False
    )

    grad_hidden = d_middle + norm_back(d_normed, first_gain, hidden, first_scale)

    def summed(received):
        return jnp.sum(received.astype(jnp.float32), axis=0)

    ff_sum = summed(ff_grads)
    out_sum = summed(out_grads)
    in_sum = summed(in_grads)
    unsplit = unsplit_grads.astype(jnp.float32).reshape(
        (ctx_size, tp_size) + unsplit_grads.shape[1:]
    )
    unsplit = jnp.sum(unsplit, axis=0)
    by_head = unsplit[..., : 2 * HEAD]
    by_head = jnp.sum(
        by_head.reshape((KVHEADS, tp_size // KVHEADS) + by_head.shape[1:]), axis=1
    )
    grad_keyval = jnp.concatenate([by_head[head] for head in range(KVHEADS)], axis=-1)
    state_vecs = jnp.sum(unsplit[..., 2 * HEAD :], axis=0)
    q_cols = q_local * HEAD
    return (
        layer_out.reshape(seq_count, row_count, width),
        grad_hidden.reshape(seq_count, row_count, width),
        small[:width],
        in_sum[:, :q_cols],
        grad_keyval,
        out_sum[:, :q_cols].T,
        in_sum[:, q_cols : q_cols + inner_local],
        out_sum[:, q_cols + inner_local :],
        state_vecs[:, :n_state],
        state_vecs[:, n_state:],
        in_sum[:, q_cols + inner_local : q_cols + inner_local + heads_local],
        head_sums[0],
        head_sums[1],
        head_sums[2],
        out_sum[:, q_cols : q_cols + inner_local].T,
        small[width : 2 * width],
        ff_sum[:, :ff_local],
        ff_sum[:, ff_local : 2 * ff_local],
        ff_sum[:, 2 * ff_local :].T,
    )


def solution(mesh):
    placed = (
        P(None, "ctx", None),
        P(),
        P(),
        P(None, "tp"),
        P(),
        P("tp", None),
        P(None, "tp"),
        P(None, "tp"),
        P(),
        P(),
        P(None, "tp"),
        P("tp"),
        P("tp"),
        P("tp"),
        P("tp", None),
        P(),
        P(None, "tp"),
        P(None, "tp"),
        P("tp", None),
        P(None, "ctx", None),
    )
    return jax.shard_map(
        body,
        mesh=mesh,
        in_specs=placed,
        out_specs=(
            P(None, "ctx", None),
            P(None, "ctx", None),
            P(),
            P("ctx", "tp"),
            P(("ctx", "tp"), None),
            P("tp", "ctx"),
            P("ctx", "tp"),
            P("ctx", "tp"),
            P(("ctx", "tp"), None),
            P(("ctx", "tp"), None),
            P("ctx", "tp"),
            P("tp"),
            P("tp"),
            P("tp"),
            P("tp", "ctx"),
            P(),
            P("ctx", "tp"),
            P("ctx", "tp"),
            P("tp", "ctx"),
        ),
        check_vma=False,
    )
```

time: 1470 us -> 568 us (0.39)
  waiting for transfers between devices: 1050 us -> 269 us
  blocking collectives: 103 us -> 39.7 us
  other arithmetic: 123 us -> 65.1 us
    reduce_scatter x8 -> x0, waiting for transfers between devices: 696 us -> none  [the longest x1 136 us: body(): lax.psum_scatter(grad_keyval, ('ctx', 'tp'), scatter_dimension=0, tiled=T...]
    unnamed x26 -> x6, waiting for transfers between devices: 200 us -> 0.1 us
    all_gather x4 -> x0, blocking collectives: 80.3 us -> none  [carried_in(): lax.all_gather(part.astype(kind), axis)]
    all_to_all x0 -> x5, waiting for transfers between devices: none -> 76 us  [spread(): return lax.all_to_all(array, axes, 0, 0, tiled=True)]
    select_n x58 -> x7, other arithmetic: 49.3 us -> 1.14 us  [the longest x2 0.9 us: block_weights(): weight = jnp.where(valid[..., None], weight, 0.0)]
    convert_element_type x47 -> x6, other arithmetic: 36 us -> 9.53 us  [the longest x2 5.3 us: weighted(): blocks[None, :, :, half].astype(jnp.float32)]
    all_to_all x0 -> x5, starting transfers between devices: none -> 23.1 us  [spread(): return lax.all_to_all(array, axes, 0, 0, tiled=True)]
    all_gather x5 -> x3, waiting for transfers between devices: 72.9 us -> 93.6 us  [the longest x1 48.3 us: body(): state_all = lax.all_gather(state.astype(jnp.bfloat16), 'ctx')]
  transfers between devices with their start and end apart: 21 -> 11, of which waited for: 19 -> 10; matrix products, arithmetic and copies ran while one was open for 15% -> 26% of each run, Pallas kernels for 0% -> 0%
where the time goes in v1:
time: 568 us; the launch traced here: 561 us
  waiting for transfers between devices  269 us (47%)
  local copies, waits for them, and re-layouts  82.4 us (15%)
  other arithmetic  65.1 us (11%)
  matrix products  65.1 us (11%)
  blocking collectives  39.7 us (7%)
  starting transfers between devices  23.7 us (4%)
  between operations  16 us (3%)
    all_to_all x5, waiting for transfers between devices, spread(): return lax.all_to_all(array, axes, 0, 0, tiled=True)  76 us
    all_gather x1, waiting for transfers between devices, body(): state_all = lax.all_gather(state.astype(jnp.bfloat16), 'ctx')  48.3 us
    psum x1, blocking collectives, body(): lax.psum(jnp.concatenate([first_part, jnp.where(tp_index == 0, grad_secon...  39.7 us
    psum x1, waiting for transfers between devices, body(): lax.psum(times_trans(d_gate_up, weights_ff).astype(jnp.bfloat16), 'tp')  36.1 us
    unnamed x274, local copies, waits for them, and re-layouts  35 us
    psum x1, waiting for transfers between devices, body(): lax.psum(d_normed_part.astype(jnp.bfloat16), 'tp').astype(jnp.float32)  34 us
    psum x1, waiting for transfers between devices, body(): lax.psum(jnp.dot(branch_in, weights_out, preferred_element_type=jnp.float...  29.2 us
    all_gather x1, waiting for transfers between devices, body(): grad_all = lax.all_gather(local_grad.astype(jnp.bfloat16), 'ctx')  24.7 us
  transfers between devices with their start and end apart: 11, of which 10 were waited for; matrix products, arithmetic and copies ran while one was open for 26% of the time, Pallas kernels for 0%

profile of v1, /device:TPU:0, one launch (start us, length us, event | category | flops | bytes accessed | tf_op | source)
XLA Modules:
  0.0 560.9 jit_solution(15733139418019618573)
XLA Ops:
  19.0 3.1 fusion.129
  49.3 20.6 %all-gather.7.cloned.1.call-done = bf16[16,144,256]{2,1,0:T(8,128)(2,1)} async-done(((bf16[2,144,256]{2,1,0:T(8,128)(2,1)}), bf16[16,144,256]{2,1,0:T(8,128)(2,1)}) %all-gather.7.cloned.1.call-update) | async-done | bytes 1179664 | tf_op jit(solution)/shard_map/all_gather | solution.py:228
  74.5 3.5 fusion.130
  83.0 48.3 %all-gather.9.cloned.1.call-done = bf16[16,2,6,64,128]{4,3,2,1,0:T(8,128)(2,1)} async-done(((bf16[2,2,6,64,128]{4,3,2,1,0:T(8,128)(2,1)}), bf16[16,2,6,64,128]{4,3,2,1,0:T(8,128)(2,1)}) %all-gather.9.cloned.1.call-update) | async-done | bytes 3145744 | tf_op jit(solution)/shard_map/all_gather | solution.py:284
  131.3 2.6 fusion.4
  142.7 2.8 convolution_convert_fusion.8
  148.3 29.2 %all-reduce.11.cloned.1.call-done = bf16[256,1024]{1,0:T(8,128)(2,1)} async-done(((bf16[256,1024]{1,0:T(8,128)(2,1)}), bf16[256,1024]{1,0:T(8,128)(2,1)}) %all-reduce.11.cloned.1.call-update) | async-done | bytes 524304 | tf_op jit(solution)/shard_map/psum | solution.py:320
  181.4 2.4 fusion.135
  185.7 3.2 convolution_convert_fusion.7
  189.2 36.1 %all-reduce.15.cloned.1.call-done = (bf16[256,1024]{1,0:T(8,128)(2,1)}, bf16[256,1024]{1,0:T(8,128)(2,1)}) async-done(((bf16[256,1024]{1,0:T(8,128)(2,1)}, bf16[256,1024]{1,0:T(8,128)(2,1)}), (bf16[256,1024]{1,0:T(8,128)(2,1)}, bf16[256,1024]{1,0:T(8,128)(2,1)})) %all-reduce.15.cloned.1.call-update) | async-done | bytes 1048592 | tf_op jit(solution)/shard_map/psum | solution.py:338
  231.7 2.5 fusion.8
  234.3 2.6 multiply_convert_fusion
  244.4 5.6 %all-to-all-start = ((bf16[8,2,128,256]{2,3,1,0:T(8,128)(2,1)}), bf16[8,2,128,256]{2,3,1,0:T(8,128)(2,1)}, u32[]{:S(2)}, u32[]{:S(2)}) async-start(bf16[8,2,128,256]{2,3,1,0:T(8,128)(2,1)} %bitcast_bitcast_fusion), calls=%async_computation | async-start | bytes 2097152 | tf_op jit(solution)/shard_map/all_to_all | solution.py:18
  255.8 32.4 %all-to-all-done = bf16[8,2,128,256]{2,3,1,0:T(8,128)(2,1)} async-done(((bf16[8,2,128,256]{2,3,1,0:T(8,128)(2,1)}), bf16[8,2,128,256]{2,3,1,0:T(8,128)(2,1)}, u32[]{:S(2)}, u32[]{:S(2)}) %all-to-all-start) | async-done | bytes 1048608 | tf_op jit(solution)/shard_map/all_to_all | solution.py:18
  288.2 4.9 all-to-all-start.4
  306.8 3.0 fusion.52
  310.6 2.6 convolution_bitcast_fusion.5
  318.7 24.7 %all-gather.11.cloned.1.call-done = bf16[16,2,6,64,128]{4,3,2,1,0:T(8,128)(2,1)} async-done(((bf16[2,2,6,64,128]{4,3,2,1,0:T(8,128)(2,1)}), bf16[16,2,6,64,128]{4,3,2,1,0:T(8,128)(2,1)}) %all-gather.11.cloned.1.call-update) | async-done | bytes 3145744 | tf_op jit(solution)/shard_map/all_gather | solution.py:376
  343.4 2.7 fusion.2
  353.8 2.6 convolution_bitcast_fusion.6
  358.2 2.5 convolution_convert_fusion.4
  360.8 22.8 %all-to-all-done.4 = bf16[8,128,1536]{1,2,0:T(8,128)(2,1)} async-done(((bf16[8,128,1536]{1,2,0:T(8,128)(2,1)}), bf16[8,128,1536]{1,2,0:T(8,128)(2,1)}, u32[]{:S(2)}, u32[]{:S(2)}) %all-to-all-start.4) | async-done | bytes 3145760 | tf_op jit(solution)/shard_map/all_to_all | solution.py:18
  383.6 3.9 all-to-all-start.2
  387.5 3.8 fusion.14
  408.7 4.9 all-to-all-done.2
  413.7 4.3 all-to-all-start.1
  421.1 2.4 convert_reduce_fusion
  438.9 15.8 %all-to-all-done.1 = bf16[8,128,768]{2,1,0:T(8,128)(2,1)} async-done(((bf16[8,128,768]{2,1,0:T(8,128)(2,1)}), bf16[8,128,768]{2,1,0:T(8,128)(2,1)}, u32[]{:S(2)}, u32[]{:S(2)}) %all-to-all-start.1) | async-done | bytes 1572896 | tf_op jit(solution)/shard_map/all_to_all | solution.py:18
  454.8 4.4 all-to-all-start.3
  459.2 4.5 fusion.132
  465.1 34.0 %all-reduce.13.cloned.1.call-done = bf16[256,1024]{1,0:T(8,128)(2,1)} async-done(((bf16[256,1024]{1,0:T(8,128)(2,1)}), bf16[256,1024]{1,0:T(8,128)(2,1)}) %all-reduce.13.cloned.1.call-update) | async-done | bytes 524304 | tf_op jit(solution)/shard_map/psum | solution.py:440
  500.8 39.7 %psum.39 = f32[2120]{0:T(1024)S(1)} all-reduce(f32[2120]{0:T(1024)S(1)} %pad_maximum_fusion.7), channel_id=1, replica_groups=mesh['ctx'=8,'tp'=4] {'ctx','tp'}, use_global_device_ids=true, to_apply=%region_34.35 | all-reduce | flops 2120 | bytes 16960 | tf_op jit(solution)/shard_map/psum | solution.py:450
  (493 shorter events, 166.6 us)
Async XLA Ops:
  7.2 176.5 %copy-start = (bf16[512,1024]{1,0:T(8,128)(2,1)S(1)}, bf16[512,1024]{1,0:T(8,128)(2,1)}, u32[]{:S(2)}) copy-start(bf16[512,1024]{1,0:T(8,128)(2,1)} %param.38) | copy-start | bytes 3145732
  7.2 62.7 %all-gather.7.cloned.1.call-start = ((), (), s32[]{:S(2)}) async-start(), calls=%async_computation.7 | async-start | bytes 1327104 | tf_op jit(solution)/shard_map/all_gather | solution.py:228
  8.1 15.3 %copy-start.117 = (f32[6]{0:T(128)}, f32[6]{0:T(128)S(1)}, u32[]{:S(2)}) copy-start(f32[6]{0:T(128)S(1)} %neg.45) | copy-start | bytes 76
  26.0 105.3 %all-gather.9.cloned.1.call-start = ((), (), s32[]{:S(2)}) async-start(), calls=%async_computation.8 | async-start | bytes 3538944 | tf_op jit(solution)/shard_map/all_gather | solution.py:284
  32.8 103.9 %copy-start.6 = (bf16[2,2,64,6,64]{2,1,0,4,3:T(2,128)(2,1)}, bf16[2,2,64,6,64]{2,1,0,4,3:T(2,128)(2,1)S(1)}, u32[]{:S(2)}) copy-start(bf16[2,2,64,6,64]{2,1,0,4,3:T(2,128)(2,1)S(1)} %reshape.669) | copy-start | bytes 589828
  32.9 102.5 %copy-start.34 = (bf16[256,128]{1,0:T(8,128)(2,1)}, bf16[256,128]{1,0:T(8,128)(2,1)S(1)}, u32[]{:S(2)}) copy-start(bf16[256,128]{1,0:T(8,128)(2,1)S(1)} %get-tuple-element.211) | copy-start | bytes 196612
  34.2 143.3 %all-reduce.11.cloned.1.call-start = ((), (), s32[]{:S(2)}) async-start(), calls=%async_computation.5 | async-start | bytes 1048576 | tf_op jit(solution)/shard_map/psum | solution.py:320
  45.2 27.8 %copy-start.23 = (bf16[640,1024]{1,0:T(8,128)(2,1)}, bf16[640,1024]{1,0:T(8,128)(2,1)S(1)}, u32[]{:S(2)}) copy-start(bf16[640,1024]{1,0:T(8,128)(2,1)S(1)} %constant_dynamic-update-slice_fusion.5) | copy-start | bytes 3932164
  145.4 79.8 %all-reduce.15.cloned.1.call-start = ((), (), s32[]{:S(2)}) async-start(), calls=%async_computation.10 | async-start | bytes 2097152 | tf_op jit(solution)/shard_map/psum | solution.py:338
  147.1 32.2 %copy-start.87 = (f32[1024]{0:T(1024)S(1)}, f32[1024]{0:T(1024)}, u32[]{:S(2)}) copy-start(f32[1024]{0:T(1024)} %param.35) | copy-start | bytes 12292
  179.3 46.0 %copy-start.96 = (f32[256]{0:T(256)}, f32[256]{0:T(256)S(1)}, u32[]{:S(2)}) copy-start(f32[256]{0:T(256)S(1)} %get-tuple-element.251) | copy-start | bytes 3076
  185.7 39.6 %copy-start.3 = (bf16[256,1024]{1,0:T(8,128)(2,1)S(1)}, bf16[256,1024]{1,0:T(8,128)(2,1)}, u32[]{:S(2)}) copy-start(bf16[256,1024]{1,0:T(8,128)(2,1)} %all-reduce.11.cloned.1.call-done) | copy-start | bytes 1572868
  188.9 38.5 %copy-start.88 = (f32[1024]{0:T(1024)S(1)}, f32[1024]{0:T(1024)}, u32[]{:S(2)}) copy-start(f32[1024]{0:T(1024)} %param.35) | copy-start | bytes 12292
  188.9 38.5 %copy-start.111 = (f32[256]{0:T(256)S(1)}, f32[256]{0:T(256)}, u32[]{:S(2)}) copy-start(f32[256]{0:T(256)} %get-tuple-element.250) | copy-start | bytes 3076
  188.9 154.5 %all-gather.11.cloned.1.call-start = ((), (), s32[]{:S(2)}) async-start(), calls=%async_computation.9 | async-start | bytes 3538944 | tf_op jit(solution)/shard_map/all_gather | solution.py:376
  244.4 43.8 %all-to-all-start = ((bf16[8,2,128,256]{2,3,1,0:T(8,128)(2,1)}), bf16[8,2,128,256]{2,3,1,0:T(8,128)(2,1)}, u32[]{:S(2)}, u32[]{:S(2)}) async-start(bf16[8,2,128,256]{2,3,1,0:T(8,128)(2,1)} %bitcast_bitcast_fusion), calls=%async_computation | async-start | bytes 2097152 | tf_op jit(solution)/shard_map/all_to_all | solution.py:18
  255.8 37.3 %copy-start.92 = (s32[2,16,1]{1,0,2:T(2,128)S(1)}, s32[2,16,1]{1,0,2:T(2,128)}, u32[]{:S(2)}) copy-start(s32[2,16,1]{1,0,2:T(2,128)} %copy-done.91) | copy-start | bytes 388
  255.8 38.4 %copy-start.105 = (s32[2,2]{1,0:T(2,128)S(1)}, s32[2,2]{1,0:T(2,128)}, u32[]{:S(2)}) copy-start(s32[2,2]{1,0:T(2,128)} %copy-done.104) | copy-start | bytes 52
  255.8 38.5 %copy-start.82 = (s32[2,2,64]{2,1,0:T(2,128)S(1)}, s32[2,2,64]{2,1,0:T(2,128)}, u32[]{:S(2)}) copy-start(s32[2,2,64]{2,1,0:T(2,128)} %copy-done.80) | copy-start | bytes 3076
  255.8 38.5 %copy-start.110 = (s32[2]{0:T(128)S(1)}, s32[2]{0:T(128)}, u32[]{:S(2)}) copy-start(s32[2]{0:T(128)} %copy-done.109) | copy-start | bytes 28
  255.8 39.2 %copy-start.120 = (pred[2,16]{1,0:T(4,128)(4,1)S(1)}, pred[2,16]{1,0:T(4,128)(4,1)}, u32[]{:S(2)}) copy-start(pred[2,16]{1,0:T(4,128)(4,1)} %get-tuple-element.257) | copy-start | bytes 100
  255.8 39.3 %copy-start.78 = (f32[15,2,6]{2,1,0:T(2,128)S(1)}, f32[15,2,6]{2,1,0:T(2,128)}, u32[]{:S(2)}) copy-start(f32[15,2,6]{2,1,0:T(2,128)} %copy-done.77) | copy-start | bytes 2164
  288.2 95.3 %all-to-all-start.4 = ((bf16[8,128,1536]{1,2,0:T(8,128)(2,1)}), bf16[8,128,1536]{1,2,0:T(8,128)(2,1)}, u32[]{:S(2)}, u32[]{:S(2)}) async-start(bf16[8,128,1536]{1,2,0:T(8,128)(2,1)} %copy_bitcast_fusion), calls=%async_computation.4 | async-start | bytes 6291456 | tf_op jit(solution)/shard_map/all_to_all | solution.py:18
  357.6 29.8 %copy-start.39 = (f32[2,2,64,64]{3,2,1,0:T(8,128)S(1)}, f32[2,2,64,64]{3,2,1,0:T(8,128)}, u32[]{:S(2)}) copy-start(f32[2,2,64,64]{3,2,1,0:T(8,128)} %fusion.134) | copy-start | bytes 196612
  383.6 30.1 %all-to-all-start.2 = ((bf16[32,32,512]{2,1,0:T(8,128)(2,1)}), bf16[32,32,512]{2,1,0:T(8,128)(2,1)}, u32[]{:S(2)}, u32[]{:S(2)}) async-start(bf16[32,32,512]{2,1,0:T(8,128)(2,1)} %bitcast.310), calls=%async_computation.2 | async-start | bytes 2097152 | tf_op jit(solution)/shard_map/all_to_all | solution.py:18
  413.7 41.1 %all-to-all-start.1 = ((bf16[8,128,768]{2,1,0:T(8,128)(2,1)}), bf16[8,128,768]{2,1,0:T(8,128)(2,1)}, u32[]{:S(2)}, u32[]{:S(2)}) async-start(bf16[8,128,768]{2,1,0:T(8,128)(2,1)} %bitcast.289), calls=%async_computation.1 | async-start | bytes 3145728 | tf_op jit(solution)/shard_map/all_to_all | solution.py:18
  454.8 95.0 %all-to-all-start.3 = ((bf16[8,128,1024]{1,2,0:T(8,128)(2,1)}), bf16[8,128,1024]{1,2,0:T(8,128)(2,1)}, u32[]{:S(2)}, u32[]{:S(2)}) async-start(bf16[8,128,1024]{1,2,0:T(8,128)(2,1)} %copy_bitcast_fusion.1), calls=%async_computation.3 | async-start | bytes 4194304 | tf_op jit(solution)/shard_map/all_to_all | solution.py:18
  459.2 39.9 %copy-start.89 = (f32[1024]{0:T(1024)S(1)}, f32[1024]{0:T(1024)}, u32[]{:S(2)}) copy-start(f32[1024]{0:T(1024)} %param.22) | copy-start | bytes 12292
  459.2 39.9 %copy-start.99 = (f32[256]{0:T(256)S(1)}, f32[256]{0:T(256)}, u32[]{:S(2)}) copy-start(f32[256]{0:T(256)} %copy-done.98) | copy-start | bytes 3076
  459.2 39.9 %all-reduce.13.cloned.1.call-start = ((), (), s32[]{:S(2)}) async-start(), calls=%async_computation.6 | async-start | bytes 1048576 | tf_op jit(solution)/shard_map/psum | solution.py:440
  463.8 78.0 %copy-start.59 = (bf16[256,1024]{1,0:T(8,128)(2,1)S(1)}, bf16[256,1024]{1,0:T(8,128)(2,1)}, u32[]{:S(2)}) copy-start(bf16[256,1024]{1,0:T(8,128)(2,1)} %get-tuple-element.21) | copy-start | bytes 1572868
  499.0 42.7 %copy-start.31 = (bf16[256,1024]{1,0:T(8,128)(2,1)S(1)}, bf16[256,1024]{1,0:T(8,128)(2,1)}, u32[]{:S(2)}) copy-start(bf16[256,1024]{1,0:T(8,128)(2,1)} %all-reduce.13.cloned.1.call-done) | copy-start | bytes 1572868
  (103 other events, 497.3 us)
Sparse Core Ops, SparseCore 0:
  26.1 43.7 all-gather.6
  72.1 59.2 all-gather.8
  145.6 31.8 all-reduce.10
  189.1 36.1 all-reduce.14
  241.6 101.7 all-gather.10
  463.9 35.0 all-reduce.12
